TPU v7x, 32 devices: a whole 2x2x4 slice. The times are simulated.
32 devices in a mesh: section: 8 (over z, x), sp: 4 (over y, core).
Axes of the slice: x: 2, y: 2, z: 4, core: 2. Of those that a mesh axis runs over, the one named last changes fastest.
Arguments:
- latents: bfloat16 [4, 64, 3072], P(None, 'sp'), may hold values from -6 to 6
- in_flight: bfloat16 [8, 64, 3072], P('section', 'sp'), may hold values from -6 to 6
- modulation: float32 [8, 3, 3072], P('section'), may hold values from -3 to 3
- w_qkv: bfloat16 [8, 3072, 3, 2048], P('section', None, None, 'sp'), may hold values from -0.109375 to 0.109375
- w_expand: bfloat16 [8, 3072, 10240], P('section', None, 'sp'), may hold values from -0.109375 to 0.109375
- qk_gain: float32 [8, 2, 128], P('section'), may hold values from 0.3 to 3
- w_out: bfloat16 [8, 2048, 3072], P('section', 'sp'), may hold values from -0.0546875 to 0.0546875
- w_contract: bfloat16 [8, 10240, 3072], P('section', 'sp'), may hold values from -0.0546875 to 0.0546875
- stale_kv: bfloat16 [8, 2, 256, 2048], P('section', None, None, 'sp'), may hold values from -400 to 400, as said below
Outputs:
- section_out: bfloat16 [8, 4, 64, 3072], P('section', None, 'sp')
- fresh_kv: bfloat16 [8, 4, 2, 64, 2048], P('section', None, None, None, 'sp')
Inputs may be any that keep to these rules, and one draw needn't show every extreme that they name: `stale_kv`: entry 0 holds keys and entry 1 values; patch m occupies rows m * 64 to (m + 1) * 64 - 1.
All inputs are finite; a program needn't handle non-finite values.
Results may differ from a plain program's by a relative error of at most 0.03.
Values may be sent and summed in bfloat16 or wider, within the bound.
No kernel may reach another device: no remote copies, remote signals or barrier semaphores. Data moves between devices by JAX's collectives and lax.ppermute only.
A program may use at most 128 MiB of HBM per device.

v0:
```python
import functools

import jax
import jax.numpy as jnp
from jax import lax
from jax.experimental import pallas as pl
from jax.experimental.pallas import tpu as pltpu
from jax.sharding import PartitionSpec as P

F32 = jnp.float32
BF16 = jnp.bfloat16
TILE = 512
EARLY = 2
FLIGHT = 4
UNIT = 256
VMEM_LIMIT = 6 * 1024 * 1024


class Places:
    def __init__(self, width, head_cols, hidden):
        self.tile = min(TILE, head_cols)
        self.width, self.head_cols, self.hidden = width, head_cols, hidden
        self.head_starts = range(0, head_cols, self.tile)
        self.hidden_starts = range(0, hidden, self.tile)
        self.width_starts = range(0, width, self.tile)
        self.rows = [0, 0, 0]
        self.qkv = [[self.take(0, width) for _ in self.head_starts] for _ in range(3)]
        self.expand = [self.take(1, width) for _ in self.hidden_starts]
        self.back = [self.take(2, head_cols + hidden) for _ in self.width_starts]

    def take(self, array, rows):
        start = self.rows[array]
        self.rows[array] += rows
        return pl.ds(start, rows)

    def columns(self, start):
        return pl.ds(start, self.tile)


def dot(left, right):
    return jnp.dot(left, right, preferred_element_type=F32)


def head_norm(values, gain_row):
    mean_square = jnp.mean(values * values, axis=-1, keepdims=True)
    return (values * lax.rsqrt(mean_square + 1e-06) * gain_row).astype(BF16)


def gelu(values):
    inner = 0.7978845608028654 * (values + 0.044715 * values * values * values)
    return (0.5 * values * (1.0 + jnp.tanh(inner))).astype(BF16)


def attend(queries, all_keys, all_values, head_dim):
    scores = lax.dot_general(
        queries, all_keys, (((1,), (1,)), ((), ())), preferred_element_type=F32
    ) * head_dim ** (-0.5)
    highest = jnp.max(scores, axis=-1, keepdims=True)
    weights = jnp.exp(scores - highest)
    totals = jnp.sum(weights, axis=-1, keepdims=True)
    shares = (weights / totals).astype(BF16)
    return dot(shares, all_values).astype(BF16)


def in_vmem(array):
    return pltpu.with_memory_space_constraint(array, pltpu.VMEM)


def in_hbm(array):
    return pltpu.with_memory_space_constraint(array, pltpu.HBM)


def load_kernel(places, w_qkv, w_expand, stale, latents, qkv, expand, back, held_stale, later, sem):
    del back
    copies = [(stale, held_stale), (latents.at[pl.ds(1, later.shape[0])], later)]
    for part, tiles in enumerate(places.qkv):
        copies += [(w_qkv.at[part, :, places.columns(c)], qkv.at[to]) for c, to in zip(places.head_starts, tiles)]
    copies += [(w_expand.at[:, places.columns(places.hidden_starts[n])], expand.at[places.expand[n]]) for n in range(EARLY)]
    copies = [pltpu.make_async_copy(*pair, sem.at[i]) for i, pair in enumerate(copies)]
    for copy in copies:
        copy.start()
    for copy in copies:
        copy.wait()


def load(places, w_qkv, w_expand, stale, latents):
    arrays = (w_qkv, w_expand, stale, latents)
    later = (latents.shape[0] - 1, *latents.shape[1:])
    nbytes = 2 * (w_qkv.size + EARLY * places.width * places.tile)
    n_copies = 2 + 3 * len(places.head_starts) + EARLY
    return pl.pallas_call(
        functools.partial(load_kernel, places),
        out_shape=[
            *(pltpu.VMEM((n, places.tile), BF16) for n in places.rows),
            pltpu.VMEM(stale.shape, BF16),
            pltpu.VMEM(later, BF16),
        ],
        in_specs=[pl.BlockSpec(memory_space=pl.ANY)] * len(arrays),
        out_specs=[pl.BlockSpec(memory_space=pltpu.VMEM)] * 5,
        scratch_shapes=[pltpu.SemaphoreType.DMA((n_copies,))],
        cost_estimate=pl.CostEstimate(flops=0, bytes_accessed=2 * nbytes, transcendentals=0),
        compiler_params=pltpu.CompilerParams(vmem_limit_bytes=VMEM_LIMIT),
        name="load",
    )(*[in_hbm(a) for a in arrays])


def on_vectors(places, gain, weights, modulated, inner, fresh, context, modulate, keep_fresh, keep_partial, arrived):
    qkv, expand, back = weights
    head_dim, head_cols, tile = gain.shape[1], places.head_cols, places.tile
    modulate(slice(0, places.width))

    def project(part, start):
        return dot(modulated[...], qkv[places.qkv[part][start // tile], :])

    def heads(start):
        return [(slice(c, c + head_dim), slice(start + c, start + c + head_dim)) for c in range(0, tile, head_dim)]

    for start in places.head_starts:
        projected = project(1, start)
        for here, columns in heads(start):
            fresh[0, :, columns] = head_norm(projected[:, here], gain[1:2, :])
        fresh[1, :, start : start + tile] = project(2, start).astype(BF16)
    keep_fresh()
    for start in places.head_starts:
        projected = project(0, start)
        for here, columns in heads(start):
            queries = head_norm(projected[:, here], gain[0:1, :])
            inner[:, columns] = attend(queries, context[0, :, columns], context[1, :, columns], head_dim)
    for number, (start, to) in enumerate(zip(places.hidden_starts, places.expand)):
        arrived(number)
        inner[:, pl.ds(head_cols + start, tile)] = gelu(dot(modulated[...], expand[to, :]))
    for number, (start, to) in enumerate(zip(places.width_starts, places.back)):
        arrived(len(places.expand) + number)
        keep_partial(start, dot(inner[...], back[to, :]).astype(BF16))


def fits_units(places, head_dim, context_rows):
    depths = (places.width, places.head_cols + places.hidden)
    wide = places.tile == places.head_cols == 2 * UNIT == 4 * head_dim
    return wide and len(places.expand) > 3 and context_rows == UNIT and all(depth % UNIT == 0 for depth in depths)


def on_units(accumulators, places, gain, weights, modulated, inner, fresh, context, modulate, keep_fresh, keep_partial, arrived):
    qkv, expand, back = weights
    head_dim, tile = gain.shape[1], places.tile
    units = range(2)
    sets = (accumulators[0:2], accumulators[2:4])
    scored = accumulators[4:6]
    patch_rows = modulated.shape[0]

    def issue(left, right, rows, into, prepare=None):
        steps = rows.size // UNIT

        def push(k, unit):
            block = right[pl.ds(rows.start + k * UNIT, UNIT), unit * UNIT : (unit + 1) * UNIT]
            pltpu.matmul_push_rhs(block, k % 2, unit)

        for unit in units:
            push(0, unit)
        for k in range(steps):
            columns = slice(k * UNIT, (k + 1) * UNIT)
            if prepare is not None:
                prepare(columns)
            piece = left[:, columns]
            for unit in units:
                if k + 1 < steps:
                    push(k + 1, unit)
                pltpu.matmul_acc_lhs(into[unit], piece, load_staged_rhs=k % 2)

    def take(into):
        return [pltpu.matmul_pop(into[unit]) for unit in units]

    def normed(halves, gain_row):
        return [head_norm(half[:, c : c + head_dim], gain_row) for half in halves for c in range(0, UNIT, head_dim)]

    def keep_activated(number, halves):
        for unit in units:
            start = places.head_cols + number * tile + unit * UNIT
            inner[:, start : start + UNIT] = gelu(halves[unit])

    issue(modulated, qkv, places.qkv[1][0], sets[0], modulate)
    issue(modulated, qkv, places.qkv[2][0], sets[1])
    for h, keys in enumerate(normed(take(sets[0]), gain[1:2, :])):
        fresh[0, :, h * head_dim : (h + 1) * head_dim] = keys
    issue(modulated, qkv, places.qkv[0][0], sets[0])
    for unit, values in enumerate(take(sets[1])):
        fresh[1, :, unit * UNIT : (unit + 1) * UNIT] = values.astype(BF16)
    keep_fresh()

    expands = len(places.expand)
    issue(modulated, expand, places.expand[0], sets[1])
    queries = normed(take(sets[0]), gain[0:1, :])
    none = jnp.zeros((patch_rows, head_dim), BF16)
    for unit in units:
        one, other = queries[2 * unit : 2 * unit + 2]
        stacked = jnp.concatenate(
            [jnp.concatenate([one, none], axis=1), jnp.concatenate([none, other], axis=1)], axis=0
        )
        pltpu.matmul_push_rhs(context[0, :, unit * UNIT : (unit + 1) * UNIT], 0, unit, transpose=True)
        pltpu.matmul_acc_lhs(scored[unit], stacked, load_staged_rhs=0)
    for number in range(1, expands):
        arrived(number)
        issue(modulated, expand, places.expand[number], sets[(number + 1) % 2])
        keep_activated(number - 1, take(sets[number % 2]))
        if number == 1:
            shares = []
            for unit in units:
                scores = pltpu.matmul_pop(scored[unit]) * head_dim ** (-0.5)
                highest = jnp.max(scores, axis=-1, keepdims=True)
                exps = jnp.exp(scores - highest)
                shares.append((exps / jnp.sum(exps, axis=-1, keepdims=True)).astype(BF16))
        if number == 2:
            for unit in units:
                pltpu.matmul_push_rhs(context[1, :, unit * UNIT : (unit + 1) * UNIT], 0, unit)
                pltpu.matmul_acc_lhs(scored[unit], shares[unit], load_staged_rhs=0)
        if number == 3:
            for unit in units:
                both = pltpu.matmul_pop(scored[unit]).astype(BF16)
                start = unit * UNIT
                inner[:, start : start + head_dim] = both[:patch_rows, :head_dim]
                inner[:, start + head_dim : start + UNIT] = both[patch_rows:, head_dim:]
    keep_activated(expands - 1, take(sets[expands % 2]))

    def keep(number):
        for unit, total in enumerate(take(sets[number % 2])):
            keep_partial(number * tile + unit * UNIT, total.astype(BF16))

    for number, rows in enumerate(places.back):
        arrived(expands + number)
        issue(inner, back, rows, sets[number % 2])
        if number > 0:
            keep(number - 1)
    keep(len(places.back) - 1)


def block_kernel(tick, micro, group, places, accumulators, *refs):
    refs = list(refs)
    n_chunks = group if tick == 0 else 2
    chunks = refs[:n_chunks]
    modulation, gain, stale, qkv, expand, back = refs[n_chunks : n_chunks + 6]
    refs = refs[n_chunks + 6 :]
    modulated, inner, fresh, context, sems = refs[-5:]
    refs = refs[:-5]
    patch_rows = modulated.shape[0]
    half = patch_rows // 2
    rows = patch_rows // group
    me = lax.axis_index("sp")
    core, order = jnp.bitwise_and(me, 1), jnp.right_shift(me, 1)
    copies, loads = [], []
    if tick == 0:
        w_expand, w_out, w_contract = refs[:3]
        partials, fresh_all, expand, back, entered = refs[3:5], *refs[5:9]
        tiles = []
        for number in range(EARLY, len(places.expand)):
            columns = places.columns(places.hidden_starts[number])
            tiles.append([(w_expand.at[:, columns], expand.at[places.expand[number]])])
        for start, to in zip(places.width_starts, places.back):
            columns = places.columns(start)
            tiles.append(
                [
                    (w_out.at[:, columns], back.at[pl.ds(to.start, places.head_cols)]),
                    (w_contract.at[:, columns], back.at[pl.ds(to.start + places.head_cols, places.hidden)]),
                ]
            )
        number = group
        for pieces in tiles:
            loads.append([pltpu.make_async_copy(*piece, sems.at[number + i]) for i, piece in enumerate(pieces)])
            number += len(pieces)
        for tile in loads[:FLIGHT]:
            for copy in tile:
                copy.start()
    else:
        result = refs[0]
        refs = refs[1 + min(tick, 2) :]
        partials, fresh_all, section_out = refs[:2], refs[2], refs[3]
        copies.append(pltpu.make_async_copy(result, section_out.at[tick - 1], sems.at[group]))
        copies[-1].start()
    patch = lax.rem(tick - lax.axis_index("section") + micro * lax.axis_size("section"), micro)
    place = pl.ds(pl.multiple_of(patch * patch_rows, patch_rows), patch_rows)

    stats = []
    for d, chunk in enumerate(chunks):
        inputs = chunk[...]
        if tick == 0:
            here = pl.multiple_of(jnp.bitwise_xor(order, d >> 1) * rows, rows)
            if d % 2 == 0:
                entered[pl.ds(here, rows), :] = inputs
            here = pl.multiple_of(here + d % 2 * half, rows)
        else:
            here = d * half
        values = inputs.astype(F32)
        average = jnp.mean(values, axis=-1, keepdims=True)
        centred = values - average
        variance = jnp.mean(centred * centred, axis=-1, keepdims=True)
        stats.append((chunk, pl.ds(here, inputs.shape[0]), average, lax.rsqrt(variance + 1e-06)))

    def modulate(columns):
        scale_row, shift_row = 1.0 + modulation[1, :, columns], modulation[0, :, columns]
        for chunk, here, average, inverse in stats:
            normed = (chunk[:, columns].astype(F32) - average) * inverse
            modulated[here, columns] = (normed * scale_row + shift_row).astype(BF16)

    context[...] = stale[...]

    def keep_fresh():
        context[:, place, :] = fresh[...]
        for d in range(group):
            owner = 2 * (d % (group // 2)) + jnp.bitwise_xor(core, d // (group // 2))
            copies.append(
                pltpu.make_async_copy(
                    fresh.at[:, pl.ds(d * rows, rows), :],
                    fresh_all.at[patch, :, pl.ds(pl.multiple_of(owner * rows, rows), rows), :],
                    sems.at[d],
                )
            )
            copies[-1].start()

    def keep_partial(start, total):
        for d in range(2):
            partials[d][:, pl.ds(start, total.shape[1])] = total[d * half : (d + 1) * half]

    def arrived(number):
        if tick > 0 or number < EARLY:
            return
        number -= EARLY
        for copy in loads[number]:
            copy.wait()
        for tile in loads[number + FLIGHT : number + FLIGHT + 1]:
            for copy in tile:
                copy.start()

    shared = (places, gain, (qkv, expand, back), modulated, inner, fresh, context, modulate, keep_fresh, keep_partial, arrived)

    def work(*into):
        if into:
            on_units(into, *shared)
        else:
            on_vectors(*shared)
        for copy in copies:
            copy.wait()

    pl.run_scoped(work, *accumulators)


def block(tick, micro, group, places, chunks, modulation, gain, stale, held, weights, result, section_out, fresh_all):
    width = chunks[0].shape[1]
    patch_rows = sum(chunk.shape[0] for chunk in chunks)
    half = jax.ShapeDtypeStruct((patch_rows // 2, width), BF16)
    vmem = pl.BlockSpec(memory_space=pltpu.VMEM)
    anywhere = pl.BlockSpec(memory_space=pl.ANY)
    out_shape = [pltpu.VMEM(half.shape, BF16)] * 2
    out_shape.append(jax.ShapeDtypeStruct((micro, 2, patch_rows, places.head_cols), BF16))
    out_specs = [vmem] * 2 + [anywhere]
    operands = [in_vmem(x) for x in (*chunks, modulation, gain, stale, *held)]
    in_specs = [vmem] * len(operands)
    aliases = {}
    n_sems = group + 1
    if tick == 0:
        aliases = {len(operands) - 2: 3, len(operands) - 1: 4}
        operands += [in_hbm(w) for w in weights]
        in_specs += [anywhere] * len(weights)
        out_shape += [pltpu.VMEM(shape, BF16) for shape in (held[1].shape, held[2].shape, half.shape)]
        out_specs += [vmem] * 3
        n_sems = group + len(places.expand) - EARLY + 2 * len(places.back)
    else:
        operands.append(in_vmem(result))
        in_specs.append(vmem)
        out_shape.append(jax.ShapeDtypeStruct((micro, patch_rows // group, width), BF16))
        out_specs.append(anywhere)
        for number, array in enumerate((fresh_all, section_out)):
            if array is not None:
                aliases[len(operands)] = 2 + number
                operands.append(in_hbm(array))
                in_specs.append(anywhere)
    accumulators = []
    if fits_units(places, gain.shape[1], stale.shape[1]):
        accumulators = [pltpu.ACC(unit)((patch_rows, UNIT), F32) for _ in range(2) for unit in range(2)]
        accumulators += [pltpu.ACC(unit)((2 * patch_rows, UNIT), F32) for unit in range(2)]
    return pl.pallas_call(
        functools.partial(block_kernel, tick, micro, group, places, accumulators),
        out_shape=out_shape,
        in_specs=in_specs,
        out_specs=out_specs,
        scratch_shapes=[
            pltpu.VMEM((patch_rows, width), BF16),
            pltpu.VMEM((patch_rows, places.head_cols + places.hidden), BF16),
            pltpu.VMEM((2, patch_rows, places.head_cols), BF16),
            pltpu.VMEM(stale.shape, BF16),
            pltpu.SemaphoreType.DMA((n_sems,)),
        ],
        input_output_aliases=aliases,
        cost_estimate=pl.CostEstimate(
            flops=2 * patch_rows * places.tile * sum(places.rows),
            bytes_accessed=2 * places.tile * sum(places.rows),
            transcendentals=patch_rows * places.hidden,
        ),
        compiler_params=pltpu.CompilerParams(vmem_limit_bytes=VMEM_LIMIT),
        name="block",
    )(*operands)


def small(kernel, name, out_shapes, operands):
    vmem = pl.BlockSpec(memory_space=pltpu.VMEM)
    return pl.pallas_call(
        kernel,
        out_shape=[pltpu.VMEM(shape, BF16) for shape in out_shapes],
        in_specs=[vmem] * len(operands),
        out_specs=[vmem] * len(out_shapes),
        compiler_params=pltpu.CompilerParams(vmem_limit_bytes=VMEM_LIMIT),
        name=name,
    )(*[in_vmem(x) for x in operands])


def place_of(distance, rows):
    order = jnp.right_shift(lax.axis_index("sp"), 1)
    return pl.ds(pl.multiple_of(jnp.bitwise_xor(order, distance) * rows, rows), rows)


def add_pair_kernel(one, other, *refs):
    chips = lax.axis_size("sp") // 2
    for e, out in enumerate(refs[-chips:]):
        rows = place_of(e, out.shape[0])
        out[...] = (one[rows, :].astype(F32) + other[rows, :].astype(F32)).astype(BF16)


def add_pair(one, other, chips):
    shape = (one.shape[0] // chips, one.shape[1])
    return small(add_pair_kernel, "add_pair", [shape] * chips, (one, other))


def finish(parts, inputs, modulation):
    total = parts[0][...].astype(F32)
    for part in parts[1:]:
        total = total + part[...].astype(F32)
    entered = inputs[place_of(0, total.shape[0]), :]
    return (entered.astype(F32) + modulation[2] * total).astype(BF16)


def finish_kernel(tick, *refs):
    *parts, inputs, modulation, later, out, leaving = refs
    result = finish(parts, inputs, modulation)
    out[...] = result
    is_last = lax.axis_index("section") == lax.axis_size("section") - 1
    leaving[...] = jnp.where(is_last, later[tick], result)


def last_kernel(tick, *refs):
    *parts, inputs, modulation, _, section_out, held, sem = refs
    held[...] = finish(parts, inputs, modulation)
    copy = pltpu.make_async_copy(held, section_out.at[tick], sem)
    copy.start()
    copy.wait()


def finish_last(tick, parts, inputs, modulation, section_out):
    vmem = pl.BlockSpec(memory_space=pltpu.VMEM)
    anywhere = pl.BlockSpec(memory_space=pl.ANY)
    operands = [in_vmem(x) for x in (*parts, inputs, modulation)]
    return pl.pallas_call(
        functools.partial(last_kernel, tick),
        out_shape=jax.ShapeDtypeStruct(section_out.shape, BF16),
        in_specs=[vmem] * len(operands) + [anywhere],
        out_specs=anywhere,
        scratch_shapes=[pltpu.VMEM(parts[0].shape, BF16), pltpu.SemaphoreType.DMA],
        input_output_aliases={len(operands): 0},
        compiler_params=pltpu.CompilerParams(vmem_limit_bytes=VMEM_LIMIT),
        name="finish_last",
    )(*operands, in_hbm(section_out))


def enter_kernel(*refs):
    *passed, out = refs
    for e, chunk in enumerate(passed):
        out[place_of(e, chunk.shape[0]), :] = chunk[...]


def swap(rows, distance):
    group = lax.axis_size("sp")
    if distance == 0:
        return rows
    return lax.ppermute(rows, "sp", [(i, i ^ distance) for i in range(group)])


def to_next_section(rows, distance):
    sections, group = lax.axis_size("section"), lax.axis_size("sp")
    route = [
        (s * group + i, (s + 1) % sections * group + (i ^ distance)) for s in range(sections) for i in range(group)
    ]
    return lax.ppermute(rows, ("section", "sp"), route)


def local(latents, in_flight, modulation, w_qkv, w_expand, qk_gain, w_out, w_contract, stale_kv):
    group = lax.axis_size("sp")
    micro = latents.shape[0]
    start = jnp.where(lax.axis_index("section") == 0, latents[0], in_flight[0])
    chunks = [swap(start, d) for d in range(group)]
    rows_modulation = jnp.transpose(modulation, (1, 0, 2))
    places = Places(w_qkv.shape[1], w_qkv.shape[3], w_expand.shape[2])
    qkv, expand, back, stale, later = load(
        places, jnp.transpose(w_qkv[0], (1, 0, 2)), w_expand[0], stale_kv[0], latents
    )
    weights = (w_expand[0], w_out[0], w_contract[0])
    chips = group // 2
    result, fresh_all, section_out = None, None, None
    for tick in range(micro):
        held = (qkv, expand, back)
        kept, sent, fresh_all, *others = block(
            tick, micro, group, places, chunks, rows_modulation, qk_gain[0], stale, held, weights, result, section_out, fresh_all
        )
        if tick == 0:
            expand, back, inputs = others
        else:
            (section_out,) = others
        sums = add_pair(kept, swap(sent, 1), chips)
        parts = [swap(sums[e], 2 * e) for e in range(chips)]
        if tick == micro - 1:
            section_out = finish_last(tick, parts, inputs, rows_modulation, section_out)
        else:
            result, leaving = small(
                functools.partial(finish_kernel, tick),
                "finish",
                [parts[0].shape] * 2,
                (*parts, inputs, rows_modulation, later),
            )
            passed = [to_next_section(leaving, 2 * e) for e in range(chips)]
            (inputs,) = small(enter_kernel, "enter", [inputs.shape], passed)
            chunks = [inputs, swap(inputs, 1)]
    return (section_out[None], fresh_all[None])


def solution(mesh):
    placed = (
        P(None, "sp", None),
        P("section", "sp", None),
        P("section", None, None),
        P("section", None, None, "sp"),
        P("section", None, "sp"),
        P("section", None, None),
        P("section", "sp", None),
        P("section", "sp", None),
        P("section", None, None, "sp"),
    )
    return jax.shard_map(
        local,
        mesh=mesh,
        in_specs=placed,
        out_specs=(P("section", None, "sp", None), P("section", None, None, None, "sp")),
        check_vma=False,
    )
```

profile of v0, /device:TPU:0, one launch (start us, length us, event | category | flops | bytes accessed | tf_op | source)
XLA Modules:
  0.0 107.7 jit_solution(13651555137502601983)
XLA Ops:
  1.6 2.5 %collective-permute-start.2 = (bf16[16,3072]{1,0:T(8,128)(2,1)S(1)}, bf16[16,3072]{1,0:T(8,128)(2,1)S(1)}, u32[]{:S(2)}, u32[]{:S(2)}) collective-permute-start(bf16[16,3072]{1,0:T(8,128)(2,1)S(1)} %select_bitcast_fusion.refs_0_), channel_id=1, source_target_pairs={{0,3},{1,2},{2,1},{3,0},{4,7},{5,6},{6,5},{7,4},{8,11},{9,10},{10,... | collective-permute-start | bytes 294920 | tf_op jit(solution)/shard_map/ppermute | solution.py:481
  4.7 5.9 %load.1 = (bf16[9216,512]{1,0:T(8,128)(2,1)S(1)}, bf16[15360,512]{1,0:T(8,128)(2,1)S(1)}, bf16[18432,512]{1,0:T(8,128)(2,1)S(1)}, bf16[2,256,512]{2,1,0:T(8,128)(2,1)S(1)}, bf16[3,16,3072]{2,1,0:T(8,128)(2,1)S(1)}) custom-call(bf16[3,3072,512]{2,1,0:T(8,128)(2,1)} %bitcast.28, bf16[3072,2560]{1,0:T(8,128)(2,1)} %bitcast.25, bf16[2,256,512]{2,1,0:T(8,128)(2,1)} %bitcast.32, ...), custom_call_target="tpu_custom_call" | custom-call | bytes 31457280 | tf_op jit(solution)/shard_map/load/pallas_call | solution.py:91
  10.7 11.0 %block.4 = (bf16[32,3072]{1,0:T(8,128)(2,1)S(1)}, bf16[32,3072]{1,0:T(8,128)(2,1)S(1)}, bf16[4,2,64,512]{3,2,1,0:T(8,128)(2,1)}, bf16[15360,512]{1,0:T(8,128)(2,...) custom-call(bf16[16,3072]{1,0:T(8,128)(2,1)S(1)} %select_bitcast_fus, ...), custom_call_target="tpu_custom_call", output_to_operand_aliasing={{3}: (8, {}), {4}: (9, {})} | custom-call | flops 2818572288 | bytes 44040192 | tf_op jit(solution)/shard_map/block/pallas_call | solution.py:379
  23.3 1.7 %collective-permute-start.4 = (bf16[16,3072]{1,0:T(8,128)(2,1)S(1)}, bf16[16,3072]{1,0:T(8,128)(2,1)S(1)}, u32[]{:S(2)}, u32[]{:S(2)}) collective-permute-start(bf16[16,3072]{1,0:T(8,128)(2,1)S(1)} %get-tuple-element.46), channel_id=1, source_target_pairs={{0,2},{1,3},{2,0},{3,1},{4,6},{5,7},{6,4},{7,5},{8,10},{9,11},{10,... | collective-permute-start | bytes 294920 | tf_op jit(solution)/shard_map/ppermute | solution.py:481
  25.0 3.4 %collective-permute-done.4.refs_1_ = bf16[16,3072]{1,0:T(8,128)(2,1)S(1)} collective-permute-done((bf16[16,3072]{1,0:T(8,128)(2,1)S(1)}, bf16[16,3072]{1,0:T(8,128)(2,1)S(1)}, u32[]{:S(2)}, u32[]{:S(2)}) %collective-permute-start.4) | collective-permute-done | bytes 98336 | tf_op jit(solution)/shard_map/ppermute | solution.py:481
  28.5 2.4 %collective-permute-start.6 = (bf16[16,3072]{1,0:T(8,128)(2,1)S(1)}, bf16[16,3072]{1,0:T(8,128)(2,1)S(1)}, u32[]{:S(2)}, u32[]{:S(2)}) collective-permute-start(bf16[16,3072]{1,0:T(8,128)(2,1)S(1)} %get-tuple-element.49), channel_id=1, source_target_pairs={{0,6},{1,7},{2,4},{3,5},{4,10},{5,11},{6,8},{7,9},{8,14},{9,15},{1... | collective-permute-start | bytes 294920 | tf_op jit(solution)/shard_map/ppermute | solution.py:489
  30.9 1.5 %collective-permute-start.5 = (bf16[16,3072]{1,0:T(8,128)(2,1)S(1)}, bf16[16,3072]{1,0:T(8,128)(2,1)S(1)}, u32[]{:S(2)}, u32[]{:S(2)}) collective-permute-start(bf16[16,3072]{1,0:T(8,128)(2,1)S(1)} %get-tuple-element.49), channel_id=1, source_target_pairs={{0,4},{1,5},{2,6},{3,7},{4,8},{5,9},{6,10},{7,11},{8,12},{9,13},{1... | collective-permute-start | bytes 294920 | tf_op jit(solution)/shard_map/ppermute | solution.py:489
  32.5 5.0 %collective-permute-done.6.refs_1_ = bf16[16,3072]{1,0:T(8,128)(2,1)S(1)} collective-permute-done((bf16[16,3072]{1,0:T(8,128)(2,1)S(1)}, bf16[16,3072]{1,0:T(8,128)(2,1)S(1)}, u32[]{:S(2)}, u32[]{:S(2)}) %collective-permute-start.6) | collective-permute-done | bytes 98336 | tf_op jit(solution)/shard_map/ppermute | solution.py:489
  38.5 1.4 %collective-permute-done.7.refs_1_ = bf16[32,3072]{1,0:T(8,128)(2,1)S(1)} collective-permute-done((bf16[32,3072]{1,0:T(8,128)(2,1)S(1)}, bf16[32,3072]{1,0:T(8,128)(2,1)S(1)}, u32[]{:S(2)}, u32[]{:S(2)}) %collective-permute-start.7) | collective-permute-done | bytes 196640 | tf_op jit(solution)/shard_map/ppermute | solution.py:481
  39.9 8.6 %block.5 = (bf16[32,3072]{1,0:T(8,128)(2,1)S(1)}, bf16[32,3072]{1,0:T(8,128)(2,1)S(1)}, bf16[4,2,64,512]{3,2,1,0:T(8,128)(2,1)}, bf16[4,16,3072]{2,1,0:T(8,128)(2,1)}) custom-call(bf16[32,3072]{1,0:T(8,128)(2,1)S(1)} %enter.3.refs_0_.refs_2_, bf16[32,3072]{1,0:T(8,128)(2,1)S(1)} %collective-permute-done.7.refs_1_, ...), custom_call_target="tpu_custom_call", output_to_operand_aliasing={{2}: (9, {})} | custom-call | flops 2818572288 | bytes 44040192 | tf_op jit(solution)/shard_map/block/pallas_call | solution.py:379
  48.7 1.3 %collective-permute-done.8.other = bf16[32,3072]{1,0:T(8,128)(2,1)S(1)} collective-permute-done((bf16[32,3072]{1,0:T(8,128)(2,1)S(1)}, bf16[32,3072]{1,0:T(8,128)(2,1)S(1)}, u32[]{:S(2)}, u32[]{:S(2)}) %collective-permute-start.8) | collective-permute-done | bytes 196640 | tf_op jit(solution)/shard_map/ppermute | solution.py:481
  50.9 4.1 %collective-permute-done.9.refs_1_ = bf16[16,3072]{1,0:T(8,128)(2,1)S(1)} collective-permute-done((bf16[16,3072]{1,0:T(8,128)(2,1)S(1)}, bf16[16,3072]{1,0:T(8,128)(2,1)S(1)}, u32[]{:S(2)}, u32[]{:S(2)}) %collective-permute-start.9) | collective-permute-done | bytes 98336 | tf_op jit(solution)/shard_map/ppermute | solution.py:481
  55.1 1.4 %collective-permute-start.10 = (bf16[16,3072]{1,0:T(8,128)(2,1)S(1)}, bf16[16,3072]{1,0:T(8,128)(2,1)S(1)}, u32[]{:S(2)}, u32[]{:S(2)}) collective-permute-start(bf16[16,3072]{1,0:T(8,128)(2,1)S(1)} %get-tuple-element.58), channel_id=1, source_target_pairs={{0,4},{1,5},{2,6},{3,7},{4,8},{5,9},{6,10},{7,11},{8,12},{9,13},{1... | collective-permute-start | bytes 294920 | tf_op jit(solution)/shard_map/ppermute | solution.py:489
  56.5 7.3 %collective-permute-done.11.refs_1_ = bf16[16,3072]{1,0:T(8,128)(2,1)S(1)} collective-permute-done((bf16[16,3072]{1,0:T(8,128)(2,1)S(1)}, bf16[16,3072]{1,0:T(8,128)(2,1)S(1)}, u32[]{:S(2)}, u32[]{:S(2)}) %collective-permute-start.11) | collective-permute-done | bytes 98336 | tf_op jit(solution)/shard_map/ppermute | solution.py:489
  64.2 1.4 %collective-permute-done.12.refs_1_ = bf16[32,3072]{1,0:T(8,128)(2,1)S(1)} collective-permute-done((bf16[32,3072]{1,0:T(8,128)(2,1)S(1)}, bf16[32,3072]{1,0:T(8,128)(2,1)S(1)}, u32[]{:S(2)}, u32[]{:S(2)}) %collective-permute-start.12) | collective-permute-done | bytes 196640 | tf_op jit(solution)/shard_map/ppermute | solution.py:481
  65.6 8.6 %block.6 = (bf16[32,3072]{1,0:T(8,128)(2,1)S(1)}, bf16[32,3072]{1,0:T(8,128)(2,1)S(1)}, bf16[4,2,64,512]{3,2,1,0:T(8,128)(2,1)}, bf16[4,16,3072]{2,1,0:T(8,128)(2,1)}) custom-call(bf16[32,3072]{1,0:T(8,128)(2,1)S(1)} %enter.4.refs_0_.refs_2_, bf16[32,3072]{1,0:T(8,128)(2,1)S(1)} %collective-permute-done.12.refs_1_, ...), custom_call_target="tpu_custom_call", output_to_operand_aliasing={{2}: (9, {}), {3}: (10, {})} | custom-call | flops 2818572288 | bytes 44040192 | tf_op jit(solution)/shard_map/block/pallas_call | solution.py:379
  74.4 1.3 %collective-permute-done.13.other = bf16[32,3072]{1,0:T(8,128)(2,1)S(1)} collective-permute-done((bf16[32,3072]{1,0:T(8,128)(2,1)S(1)}, bf16[32,3072]{1,0:T(8,128)(2,1)S(1)}, u32[]{:S(2)}, u32[]{:S(2)}) %collective-permute-start.13) | collective-permute-done | bytes 196640 | tf_op jit(solution)/shard_map/ppermute | solution.py:481
  75.7 1.4 %collective-permute-start.14 = (bf16[16,3072]{1,0:T(8,128)(2,1)S(1)}, bf16[16,3072]{1,0:T(8,128)(2,1)S(1)}, u32[]{:S(2)}, u32[]{:S(2)}) collective-permute-start(bf16[16,3072]{1,0:T(8,128)(2,1)S(1)} %get-tuple-element.65), channel_id=1, source_target_pairs={{0,2},{1,3},{2,0},{3,1},{4,6},{5,7},{6,4},{7,5},{8,10},{9,11},{10,... | collective-permute-start | bytes 294920 | tf_op jit(solution)/shard_map/ppermute | solution.py:481
  77.1 3.5 %collective-permute-done.14.refs_1_ = bf16[16,3072]{1,0:T(8,128)(2,1)S(1)} collective-permute-done((bf16[16,3072]{1,0:T(8,128)(2,1)S(1)}, bf16[16,3072]{1,0:T(8,128)(2,1)S(1)}, u32[]{:S(2)}, u32[]{:S(2)}) %collective-permute-start.14) | collective-permute-done | bytes 98336 | tf_op jit(solution)/shard_map/ppermute | solution.py:481
  80.9 8.5 %collective-permute-done.16.refs_1_ = bf16[16,3072]{1,0:T(8,128)(2,1)S(1)} collective-permute-done((bf16[16,3072]{1,0:T(8,128)(2,1)S(1)}, bf16[16,3072]{1,0:T(8,128)(2,1)S(1)}, u32[]{:S(2)}, u32[]{:S(2)}) %collective-permute-start.16) | collective-permute-done | bytes 98336 | tf_op jit(solution)/shard_map/ppermute | solution.py:489
  90.4 1.4 %collective-permute-done.17.refs_1_ = bf16[32,3072]{1,0:T(8,128)(2,1)S(1)} collective-permute-done((bf16[32,3072]{1,0:T(8,128)(2,1)S(1)}, bf16[32,3072]{1,0:T(8,128)(2,1)S(1)}, u32[]{:S(2)}, u32[]{:S(2)}) %collective-permute-start.17) | collective-permute-done | bytes 196640 | tf_op jit(solution)/shard_map/ppermute | solution.py:481
  91.8 8.6 %block.7 = (bf16[32,3072]{1,0:T(8,128)(2,1)S(1)}, bf16[32,3072]{1,0:T(8,128)(2,1)S(1)}, bf16[4,2,64,512]{3,2,1,0:T(8,128)(2,1)}, bf16[4,16,3072]{2,1,0:T(8,128)(2,1)}) custom-call(bf16[32,3072]{1,0:T(8,128)(2,1)S(1)} %enter.5.refs_0_.refs_2_, bf16[32,3072]{1,0:T(8,128)(2,1)S(1)} %collective-permute-done.17.refs_1_, ...), custom_call_target="tpu_custom_call", output_to_operand_aliasing={{2}: (9, {}), {3}: (10, {})} | custom-call | flops 2818572288 | bytes 44040192 | tf_op jit(solution)/shard_map/block/pallas_call | solution.py:379
  100.6 1.3 %collective-permute-done.18.other = bf16[32,3072]{1,0:T(8,128)(2,1)S(1)} collective-permute-done((bf16[32,3072]{1,0:T(8,128)(2,1)S(1)}, bf16[32,3072]{1,0:T(8,128)(2,1)S(1)}, u32[]{:S(2)}, u32[]{:S(2)}) %collective-permute-start.18) | collective-permute-done | bytes 196640 | tf_op jit(solution)/shard_map/ppermute | solution.py:481
  102.7 4.1 %collective-permute-done.19.refs_1_ = bf16[16,3072]{1,0:T(8,128)(2,1)S(1)} collective-permute-done((bf16[16,3072]{1,0:T(8,128)(2,1)S(1)}, bf16[16,3072]{1,0:T(8,128)(2,1)S(1)}, u32[]{:S(2)}, u32[]{:S(2)}) %collective-permute-start.19) | collective-permute-done | bytes 98336 | tf_op jit(solution)/shard_map/ppermute | solution.py:481
  (37 shorter events, 9.1 us)
Async XLA Ops:
  0.6 10.0 %copy-start.1 = (f32[1,2,128]{2,1,0:T(2,128)S(1)}, f32[1,2,128]{2,1,0:T(2,128)}, u32[]{:S(2)}) copy-start(f32[1,2,128]{2,1,0:T(2,128)} %param.14) | copy-start | bytes 3076
  0.6 10.0 %copy-start = (f32[1,3,3072]{2,0,1:T(1,128)S(1)}, f32[1,3,3072]{2,0,1:T(1,128)}, u32[]{:S(2)}) copy-start(f32[1,3,3072]{2,0,1:T(1,128)} %param.11) | copy-start | bytes 110596
  1.6 9.0 %collective-permute-start.2 = (bf16[16,3072]{1,0:T(8,128)(2,1)S(1)}, bf16[16,3072]{1,0:T(8,128)(2,1)S(1)}, u32[]{:S(2)}, u32[]{:S(2)}) collective-permute-start(bf16[16,3072]{1,0:T(8,128)(2,1)S(1)} %select_bitcast_fusion.refs_0_), channel_id=1, source_target_pairs={{0,3},{1,2},{2,1},{3,0},{4,7},{5,6},{6,5},{7,4},{8,11},{9,10},{10,... | collective-permute-start | bytes 294920 | tf_op jit(solution)/shard_map/ppermute | solution.py:481
  4.0 6.6 %collective-permute-start.1 = (bf16[16,3072]{1,0:T(8,128)(2,1)S(1)}, bf16[16,3072]{1,0:T(8,128)(2,1)S(1)}, u32[]{:S(2)}, u32[]{:S(2)}) collective-permute-start(bf16[16,3072]{1,0:T(8,128)(2,1)S(1)} %select_bitcast_fusion.refs_0_), channel_id=1, source_target_pairs={{0,2},{1,3},{2,0},{3,1},{4,6},{5,7},{6,4},{7,5},{8,10},{9,11},{10,... | collective-permute-start | bytes 294920 | tf_op jit(solution)/shard_map/ppermute | solution.py:481
  4.7 5.9 %collective-permute-start = (bf16[16,3072]{1,0:T(8,128)(2,1)S(1)}, bf16[16,3072]{1,0:T(8,128)(2,1)S(1)}, u32[]{:S(2)}, u32[]{:S(2)}) collective-permute-start(bf16[16,3072]{1,0:T(8,128)(2,1)S(1)} %select_bitcast_fusion.refs_0_), channel_id=1, source_target_pairs={{0,1},{1,0},{2,3},{3,2},{4,5},{5,4},{6,7},{7,6},{8,9},{9,8},{10,11... | collective-permute-start | bytes 294920 | tf_op jit(solution)/shard_map/ppermute | solution.py:481
  21.6 1.6 %collective-permute-start.3 = (bf16[32,3072]{1,0:T(8,128)(2,1)S(1)}, bf16[32,3072]{1,0:T(8,128)(2,1)S(1)}, u32[]{:S(2)}, u32[]{:S(2)}) collective-permute-start(bf16[32,3072]{1,0:T(8,128)(2,1)S(1)} %get-tuple-element.44), channel_id=1, source_target_pairs={{0,1},{1,0},{2,3},{3,2},{4,5},{5,4},{6,7},{7,6},{8,9},{9,8},{10,11... | collective-permute-start | bytes 589832 | tf_op jit(solution)/shard_map/ppermute | solution.py:481
  23.3 5.1 %collective-permute-start.4 = (bf16[16,3072]{1,0:T(8,128)(2,1)S(1)}, bf16[16,3072]{1,0:T(8,128)(2,1)S(1)}, u32[]{:S(2)}, u32[]{:S(2)}) collective-permute-start(bf16[16,3072]{1,0:T(8,128)(2,1)S(1)} %get-tuple-element.46), channel_id=1, source_target_pairs={{0,2},{1,3},{2,0},{3,1},{4,6},{5,7},{6,4},{7,5},{8,10},{9,11},{10,... | collective-permute-start | bytes 294920 | tf_op jit(solution)/shard_map/ppermute | solution.py:481
  28.5 9.0 %collective-permute-start.6 = (bf16[16,3072]{1,0:T(8,128)(2,1)S(1)}, bf16[16,3072]{1,0:T(8,128)(2,1)S(1)}, u32[]{:S(2)}, u32[]{:S(2)}) collective-permute-start(bf16[16,3072]{1,0:T(8,128)(2,1)S(1)} %get-tuple-element.49), channel_id=1, source_target_pairs={{0,6},{1,7},{2,4},{3,5},{4,10},{5,11},{6,8},{7,9},{8,14},{9,15},{1... | collective-permute-start | bytes 294920 | tf_op jit(solution)/shard_map/ppermute | solution.py:489
  30.9 7.5 %collective-permute-start.5 = (bf16[16,3072]{1,0:T(8,128)(2,1)S(1)}, bf16[16,3072]{1,0:T(8,128)(2,1)S(1)}, u32[]{:S(2)}, u32[]{:S(2)}) collective-permute-start(bf16[16,3072]{1,0:T(8,128)(2,1)S(1)} %get-tuple-element.49), channel_id=1, source_target_pairs={{0,4},{1,5},{2,6},{3,7},{4,8},{5,9},{6,10},{7,11},{8,12},{9,13},{1... | collective-permute-start | bytes 294920 | tf_op jit(solution)/shard_map/ppermute | solution.py:489
  38.4 1.5 %collective-permute-start.7 = (bf16[32,3072]{1,0:T(8,128)(2,1)S(1)}, bf16[32,3072]{1,0:T(8,128)(2,1)S(1)}, u32[]{:S(2)}, u32[]{:S(2)}) collective-permute-start(bf16[32,3072]{1,0:T(8,128)(2,1)S(1)} %enter.3.refs_0_.refs_2_), channel_id=1, source_target_pairs={{0,1},{1,0},{2,3},{3,2},{4,5},{5,4},{6,7},{7,6},{8,9},{9,8},{10,11... | collective-permute-start | bytes 589832 | tf_op jit(solution)/shard_map/ppermute | solution.py:481
  48.5 1.5 %collective-permute-start.8 = (bf16[32,3072]{1,0:T(8,128)(2,1)S(1)}, bf16[32,3072]{1,0:T(8,128)(2,1)S(1)}, u32[]{:S(2)}, u32[]{:S(2)}) collective-permute-start(bf16[32,3072]{1,0:T(8,128)(2,1)S(1)} %get-tuple-element.55), channel_id=1, source_target_pairs={{0,1},{1,0},{2,3},{3,2},{4,5},{5,4},{6,7},{7,6},{8,9},{9,8},{10,11... | collective-permute-start | bytes 589832 | tf_op jit(solution)/shard_map/ppermute | solution.py:481
  50.1 4.9 %collective-permute-start.9 = (bf16[16,3072]{1,0:T(8,128)(2,1)S(1)}, bf16[16,3072]{1,0:T(8,128)(2,1)S(1)}, u32[]{:S(2)}, u32[]{:S(2)}) collective-permute-start(bf16[16,3072]{1,0:T(8,128)(2,1)S(1)} %get-tuple-element.57), channel_id=1, source_target_pairs={{0,2},{1,3},{2,0},{3,1},{4,6},{5,7},{6,4},{7,5},{8,10},{9,11},{10,... | collective-permute-start | bytes 294920 | tf_op jit(solution)/shard_map/ppermute | solution.py:481
  55.0 8.7 %collective-permute-start.11 = (bf16[16,3072]{1,0:T(8,128)(2,1)S(1)}, bf16[16,3072]{1,0:T(8,128)(2,1)S(1)}, u32[]{:S(2)}, u32[]{:S(2)}) collective-permute-start(bf16[16,3072]{1,0:T(8,128)(2,1)S(1)} %get-tuple-element.58), channel_id=1, source_target_pairs={{0,6},{1,7},{2,4},{3,5},{4,10},{5,11},{6,8},{7,9},{8,14},{9,15},{1... | collective-permute-start | bytes 294920 | tf_op jit(solution)/shard_map/ppermute | solution.py:489
  55.1 9.0 %collective-permute-start.10 = (bf16[16,3072]{1,0:T(8,128)(2,1)S(1)}, bf16[16,3072]{1,0:T(8,128)(2,1)S(1)}, u32[]{:S(2)}, u32[]{:S(2)}) collective-permute-start(bf16[16,3072]{1,0:T(8,128)(2,1)S(1)} %get-tuple-element.58), channel_id=1, source_target_pairs={{0,4},{1,5},{2,6},{3,7},{4,8},{5,9},{6,10},{7,11},{8,12},{9,13},{1... | collective-permute-start | bytes 294920 | tf_op jit(solution)/shard_map/ppermute | solution.py:489
  64.1 1.5 %collective-permute-start.12 = (bf16[32,3072]{1,0:T(8,128)(2,1)S(1)}, bf16[32,3072]{1,0:T(8,128)(2,1)S(1)}, u32[]{:S(2)}, u32[]{:S(2)}) collective-permute-start(bf16[32,3072]{1,0:T(8,128)(2,1)S(1)} %enter.4.refs_0_.refs_2_), channel_id=1, source_target_pairs={{0,1},{1,0},{2,3},{3,2},{4,5},{5,4},{6,7},{7,6},{8,9},{9,8},{10,11... | collective-permute-start | bytes 589832 | tf_op jit(solution)/shard_map/ppermute | solution.py:481
  74.2 1.5 %collective-permute-start.13 = (bf16[32,3072]{1,0:T(8,128)(2,1)S(1)}, bf16[32,3072]{1,0:T(8,128)(2,1)S(1)}, u32[]{:S(2)}, u32[]{:S(2)}) collective-permute-start(bf16[32,3072]{1,0:T(8,128)(2,1)S(1)} %get-tuple-element.63), channel_id=1, source_target_pairs={{0,1},{1,0},{2,3},{3,2},{4,5},{5,4},{6,7},{7,6},{8,9},{9,8},{10,11... | collective-permute-start | bytes 589832 | tf_op jit(solution)/shard_map/ppermute | solution.py:481
  75.7 4.9 %collective-permute-start.14 = (bf16[16,3072]{1,0:T(8,128)(2,1)S(1)}, bf16[16,3072]{1,0:T(8,128)(2,1)S(1)}, u32[]{:S(2)}, u32[]{:S(2)}) collective-permute-start(bf16[16,3072]{1,0:T(8,128)(2,1)S(1)} %get-tuple-element.65), channel_id=1, source_target_pairs={{0,2},{1,3},{2,0},{3,1},{4,6},{5,7},{6,4},{7,5},{8,10},{9,11},{10,... | collective-permute-start | bytes 294920 | tf_op jit(solution)/shard_map/ppermute | solution.py:481
  80.7 8.7 %collective-permute-start.16 = (bf16[16,3072]{1,0:T(8,128)(2,1)S(1)}, bf16[16,3072]{1,0:T(8,128)(2,1)S(1)}, u32[]{:S(2)}, u32[]{:S(2)}) collective-permute-start(bf16[16,3072]{1,0:T(8,128)(2,1)S(1)} %get-tuple-element.66), channel_id=1, source_target_pairs={{0,6},{1,7},{2,4},{3,5},{4,10},{5,11},{6,8},{7,9},{8,14},{9,15},{1... | collective-permute-start | bytes 294920 | tf_op jit(solution)/shard_map/ppermute | solution.py:489
  80.7 9.5 %collective-permute-start.15 = (bf16[16,3072]{1,0:T(8,128)(2,1)S(1)}, bf16[16,3072]{1,0:T(8,128)(2,1)S(1)}, u32[]{:S(2)}, u32[]{:S(2)}) collective-permute-start(bf16[16,3072]{1,0:T(8,128)(2,1)S(1)} %get-tuple-element.66), channel_id=1, source_target_pairs={{0,4},{1,5},{2,6},{3,7},{4,8},{5,9},{6,10},{7,11},{8,12},{9,13},{1... | collective-permute-start | bytes 294920 | tf_op jit(solution)/shard_map/ppermute | solution.py:489
  90.3 1.5 %collective-permute-start.17 = (bf16[32,3072]{1,0:T(8,128)(2,1)S(1)}, bf16[32,3072]{1,0:T(8,128)(2,1)S(1)}, u32[]{:S(2)}, u32[]{:S(2)}) collective-permute-start(bf16[32,3072]{1,0:T(8,128)(2,1)S(1)} %enter.5.refs_0_.refs_2_), channel_id=1, source_target_pairs={{0,1},{1,0},{2,3},{3,2},{4,5},{5,4},{6,7},{7,6},{8,9},{9,8},{10,11... | collective-permute-start | bytes 589832 | tf_op jit(solution)/shard_map/ppermute | solution.py:481
  100.4 1.5 %collective-permute-start.18 = (bf16[32,3072]{1,0:T(8,128)(2,1)S(1)}, bf16[32,3072]{1,0:T(8,128)(2,1)S(1)}, u32[]{:S(2)}, u32[]{:S(2)}) collective-permute-start(bf16[32,3072]{1,0:T(8,128)(2,1)S(1)} %get-tuple-element.71), channel_id=1, source_target_pairs={{0,1},{1,0},{2,3},{3,2},{4,5},{5,4},{6,7},{7,6},{8,9},{9,8},{10,11... | collective-permute-start | bytes 589832 | tf_op jit(solution)/shard_map/ppermute | solution.py:481
  101.9 4.9 %collective-permute-start.19 = (bf16[16,3072]{1,0:T(8,128)(2,1)S(1)}, bf16[16,3072]{1,0:T(8,128)(2,1)S(1)}, u32[]{:S(2)}, u32[]{:S(2)}) collective-permute-start(bf16[16,3072]{1,0:T(8,128)(2,1)S(1)} %get-tuple-element.73), channel_id=1, source_target_pairs={{0,2},{1,3},{2,0},{3,1},{4,6},{5,7},{6,4},{7,5},{8,10},{9,11},{10,... | collective-permute-start | bytes 294920 | tf_op jit(solution)/shard_map/ppermute | solution.py:481
where the time goes:
time: 108 us
  waiting for transfers between devices  47.3 us (44%)
  Pallas kernels  43.6 us (40%)
  starting transfers between devices  14.8 us (14%)
    pallas_call x4, Pallas kernels, block(): pl.pallas_call(functools.partial(block_kernel, tick, micro, group, places...  36.7 us
    ppermute x14, waiting for transfers between devices, swap(): return lax.ppermute(rows, 'sp', [(i, i ^ distance) for i in range(group)])  24.5 us
    ppermute x6, waiting for transfers between devices, to_next_section(): return lax.ppermute(rows, ('section', 'sp'), route)  22.9 us
    ppermute x14, starting transfers between devices, swap(): return lax.ppermute(rows, 'sp', [(i, i ^ distance) for i in range(group)])  9.17 us
    pallas_call x1, Pallas kernels, load(): pl.pallas_call(functools.partial(load_kernel, places), out_shape=[*(pltpu...  5.87 us
    ppermute x6, starting transfers between devices, to_next_section(): return lax.ppermute(rows, ('section', 'sp'), route)  5.66 us
  transfers between devices with their start and end apart: 20, of which 17 were waited for; matrix products, arithmetic and copies ran while one was open for 0% of the time, Pallas kernels for 5%

commit v1 on v0

--- a/solution.py
+++ b/solution.py
@@ -399,16 +399,16 @@
     )(*operands)
 
 
-def small(kernel, name, out_shapes, operands):
+def small(kernel, name, out_shapes, operands, unused=()):
     vmem = pl.BlockSpec(memory_space=pltpu.VMEM)
     return pl.pallas_call(
         kernel,
         out_shape=[pltpu.VMEM(shape, BF16) for shape in out_shapes],
-        in_specs=[vmem] * len(operands),
+        in_specs=[vmem] * len(operands) + [pl.BlockSpec(memory_space=pl.ANY)] * len(unused),
         out_specs=[vmem] * len(out_shapes),
         compiler_params=pltpu.CompilerParams(vmem_limit_bytes=VMEM_LIMIT),
         name=name,
-    )(*[in_vmem(x) for x in operands])
+    )(*[in_vmem(x) for x in operands], *unused)
 
 
 def place_of(distance, rows):
@@ -423,9 +423,9 @@
         out[...] = (one[rows, :].astype(F32) + other[rows, :].astype(F32)).astype(BF16)
 
 
-def add_pair(one, other, chips):
+def add_pair(one, other, chips, unused):
     shape = (one.shape[0] // chips, one.shape[1])
-    return small(add_pair_kernel, "add_pair", [shape] * chips, (one, other))
+    return small(add_pair_kernel, "add_pair", [shape] * chips, (one, other), unused)
 
 
 def finish(parts, inputs, modulation):
@@ -436,12 +436,9 @@
     return (entered.astype(F32) + modulation[2] * total).astype(BF16)
 
 
-def finish_kernel(tick, *refs):
-    *parts, inputs, modulation, later, out, leaving = refs
-    result = finish(parts, inputs, modulation)
-    out[...] = result
-    is_last = lax.axis_index("section") == lax.axis_size("section") - 1
-    leaving[...] = jnp.where(is_last, later[tick], result)
+def finish_kernel(*refs):
+    *parts, inputs, modulation, out = refs
+    out[...] = finish(parts, inputs, modulation)
 
 
 def last_kernel(tick, *refs):
@@ -468,10 +465,13 @@
     )(*operands, in_hbm(section_out))
 
 
-def enter_kernel(*refs):
-    *passed, out = refs
-    for e, chunk in enumerate(passed):
-        out[place_of(e, chunk.shape[0]), :] = chunk[...]
+def enter_kernel(tick, *refs):
+    chips = len(refs) // 2
+    passed, early, out = refs[:chips], refs[chips : 2 * chips], refs[-1]
+    rows = passed[0].shape[0]
+    is_first = lax.axis_index("section") == 0
+    for e in range(chips):
+        out[place_of(e, rows), :] = jnp.where(is_first, early[e][tick], passed[e][...])
 
 
 def swap(rows, distance):
@@ -483,9 +483,8 @@
 
 def to_next_section(rows, distance):
     sections, group = lax.axis_size("section"), lax.axis_size("sp")
-    route = [
-        (s * group + i, (s + 1) % sections * group + (i ^ distance)) for s in range(sections) for i in range(group)
-    ]
+    route = [(s * group + i, (s + 1) * group + (i ^ distance)) for s in range(sections - 1) for i in range(group)]
+    route += [((sections - 1) * group + i, i) for i in range(group)]
     return lax.ppermute(rows, ("section", "sp"), route)
 
 
@@ -501,6 +500,7 @@
     )
     weights = (w_expand[0], w_out[0], w_contract[0])
     chips = group // 2
+    early = [swap(later, 2 * e) for e in range(chips)]
     result, fresh_all, section_out = None, None, None
     for tick in range(micro):
         held = (qkv, expand, back)
@@ -511,19 +511,14 @@
             expand, back, inputs = others
         else:
             (section_out,) = others
-        sums = add_pair(kept, swap(sent, 1), chips)
+        sums = add_pair(kept, swap(sent, 1), chips, early[1:] if tick == 0 else ())
         parts = [swap(sums[e], 2 * e) for e in range(chips)]
         if tick == micro - 1:
             section_out = finish_last(tick, parts, inputs, rows_modulation, section_out)
         else:
-            result, leaving = small(
-                functools.partial(finish_kernel, tick),
-                "finish",
-                [parts[0].shape] * 2,
-                (*parts, inputs, rows_modulation, later),
-            )
-            passed = [to_next_section(leaving, 2 * e) for e in range(chips)]
-            (inputs,) = small(enter_kernel, "enter", [inputs.shape], passed)
+            (result,) = small(finish_kernel, "finish", [parts[0].shape], (*parts, inputs, rows_modulation))
+            passed = [to_next_section(result, 2 * e) for e in range(chips)]
+            (inputs,) = small(functools.partial(enter_kernel, tick), "enter", [inputs.shape], (*passed, *early))
             chunks = [inputs, swap(inputs, 1)]
     return (section_out[None], fresh_all[None])
 

time: 108 us -> 108 us (level)
    ppermute x14 -> x15, waiting for transfers between devices: 24.5 us -> 27.1 us  [swap(): return lax.ppermute(rows, 'sp', [(i, i ^ distance) for i in range(group)])]
    ppermute x6, waiting for transfers between devices: 22.9 us -> 20.5 us  [to_next_section(): return lax.ppermute(rows, ('section', 'sp'), route)]
    ppermute x14 -> x15, starting transfers between devices: 9.17 us -> 8.02 us  [swap(): return lax.ppermute(rows, 'sp', [(i, i ^ distance) for i in range(group)])]
  transfers between devices with their start and end apart: 20 -> 21, of which waited for: 17 -> 17; matrix products, arithmetic and copies ran while one was open for 0% -> 0% of each run, Pallas kernels for 5% -> 16%
where the time goes in v1:
time: 108 us
  waiting for transfers between devices  47.6 us (44%)
  Pallas kernels  43.6 us (40%)
  starting transfers between devices  14.5 us (13%)
    pallas_call x4, Pallas kernels, block(): pl.pallas_call(functools.partial(block_kernel, tick, micro, group, places...  36.6 us
    ppermute x15, waiting for transfers between devices, swap(): return lax.ppermute(rows, 'sp', [(i, i ^ distance) for i in range(group)])  27.1 us
    ppermute x6, waiting for transfers between devices, to_next_section(): return lax.ppermute(rows, ('section', 'sp'), route)  20.5 us
    ppermute x15, starting transfers between devices, swap(): return lax.ppermute(rows, 'sp', [(i, i ^ distance) for i in range(group)])  8.02 us
    ppermute x6, starting transfers between devices, to_next_section(): return lax.ppermute(rows, ('section', 'sp'), route)  6.51 us
    pallas_call x1, Pallas kernels, load(): pl.pallas_call(functools.partial(load_kernel, places), out_shape=[*(pltpu...  5.87 us
  transfers between devices with their start and end apart: 21, of which 17 were waited for; matrix products, arithmetic and copies ran while one was open for 0% of the time, Pallas kernels for 16%

profile of v1, /device:TPU:0, one launch (start us, length us, event | category | flops | bytes accessed | tf_op | source)
XLA Modules:
  0.0 107.6 jit_solution(495053113714317949)
XLA Ops:
  2.1 2.6 %collective-permute-start.1 = (bf16[16,3072]{1,0:T(8,128)(2,1)S(1)}, bf16[16,3072]{1,0:T(8,128)(2,1)S(1)}, u32[]{:S(2)}, u32[]{:S(2)}) collective-permute-start(bf16[16,3072]{1,0:T(8,128)(2,1)S(1)} %select_bitcast_fusion.refs_0_), channel_id=1, source_target_pairs={{0,2},{1,3},{2,0},{3,1},{4,6},{5,7},{6,4},{7,5},{8,10},{9,11},{10,... | collective-permute-start | bytes 294920 | tf_op jit(solution)/shard_map/ppermute | solution.py:481
  4.8 5.9 %load.1 = (bf16[9216,512]{1,0:T(8,128)(2,1)S(1)}, bf16[15360,512]{1,0:T(8,128)(2,1)S(1)}, bf16[18432,512]{1,0:T(8,128)(2,1)S(1)}, bf16[2,256,512]{2,1,0:T(8,128)(2,1)S(1)}, bf16[3,16,3072]{2,1,0:T(8,128)(2,1)S(1)}) custom-call(bf16[3,3072,512]{2,1,0:T(8,128)(2,1)} %bitcast.28, bf16[3072,2560]{1,0:T(8,128)(2,1)} %bitcast.25, bf16[2,256,512]{2,1,0:T(8,128)(2,1)} %bitcast.32, ...), custom_call_target="tpu_custom_call" | custom-call | bytes 31457280 | tf_op jit(solution)/shard_map/load/pallas_call | solution.py:91
  10.6 1.8 %collective-permute-start.4 = (bf16[3,16,3072]{2,1,0:T(8,128)(2,1)S(1)}, bf16[3,16,3072]{2,1,0:T(8,128)(2,1)S(1)}, u32[]{:S(2)}, u32[]{:S(2)}) collective-permute-start(bf16[3,16,3072]{2,1,0:T(8,128)(2,1)S(1)} %get-tuple-element.39.refs_2_), channel_id=1, source_target_pairs={{0,2},{1,3},{2,0},{3,1},{4,6},{5,7},{6,4},{7,5},{8,10},{9,11},{10,... | collective-permute-start | bytes 884744 | tf_op jit(solution)/shard_map/ppermute | solution.py:481
  12.5 11.0 %block.4 = (bf16[32,3072]{1,0:T(8,128)(2,1)S(1)}, bf16[32,3072]{1,0:T(8,128)(2,1)S(1)}, bf16[4,2,64,512]{3,2,1,0:T(8,128)(2,1)}, bf16[15360,512]{1,0:T(8,128)(2,...) custom-call(bf16[16,3072]{1,0:T(8,128)(2,1)S(1)} %select_bitcast_fus, ...), custom_call_target="tpu_custom_call", output_to_operand_aliasing={{3}: (8, {}), {4}: (9, {})} | custom-call | flops 2818572288 | bytes 44040192 | tf_op jit(solution)/shard_map/block/pallas_call | solution.py:379
  23.6 1.4 %collective-permute-done.3.other = bf16[32,3072]{1,0:T(8,128)(2,1)S(1)} collective-permute-done((bf16[32,3072]{1,0:T(8,128)(2,1)S(1)}, bf16[32,3072]{1,0:T(8,128)(2,1)S(1)}, u32[]{:S(2)}, u32[]{:S(2)}) %collective-permute-start.3) | collective-permute-done | bytes 196640 | tf_op jit(solution)/shard_map/ppermute | solution.py:481
  25.4 4.5 %collective-permute-done.5.refs_1_ = bf16[16,3072]{1,0:T(8,128)(2,1)S(1)} collective-permute-done((bf16[16,3072]{1,0:T(8,128)(2,1)S(1)}, bf16[16,3072]{1,0:T(8,128)(2,1)S(1)}, u32[]{:S(2)}, u32[]{:S(2)}) %collective-permute-start.5) | collective-permute-done | bytes 98336 | tf_op jit(solution)/shard_map/ppermute | solution.py:481
  30.0 1.6 %collective-permute-start.6 = (bf16[16,3072]{1,0:T(8,128)(2,1)S(1)}, bf16[16,3072]{1,0:T(8,128)(2,1)S(1)}, u32[]{:S(2)}, u32[]{:S(2)}) collective-permute-start(bf16[16,3072]{1,0:T(8,128)(2,1)S(1)} %finish.3.refs_8_), channel_id=1, source_target_pairs={{0,4},{1,5},{2,6},{3,7},{4,8},{5,9},{6,10},{7,11},{8,12},{9,13},{1... | collective-permute-start | bytes 294920 | tf_op jit(solution)/shard_map/ppermute | solution.py:488
  31.6 1.5 %collective-permute-start.7 = (bf16[16,3072]{1,0:T(8,128)(2,1)S(1)}, bf16[16,3072]{1,0:T(8,128)(2,1)S(1)}, u32[]{:S(2)}, u32[]{:S(2)}) collective-permute-start(bf16[16,3072]{1,0:T(8,128)(2,1)S(1)} %finish.3.refs_8_), channel_id=1, source_target_pairs={{0,6},{1,7},{2,4},{3,5},{4,10},{5,11},{6,8},{7,9},{8,14},{9,15},{1... | collective-permute-start | bytes 294920 | tf_op jit(solution)/shard_map/ppermute | solution.py:488
  33.0 4.9 %collective-permute-done.6.refs_0_ = bf16[16,3072]{1,0:T(8,128)(2,1)S(1)} collective-permute-done((bf16[16,3072]{1,0:T(8,128)(2,1)S(1)}, bf16[16,3072]{1,0:T(8,128)(2,1)S(1)}, u32[]{:S(2)}, u32[]{:S(2)}) %collective-permute-start.6) | collective-permute-done | bytes 98336 | tf_op jit(solution)/shard_map/ppermute | solution.py:488
  39.1 1.4 %collective-permute-done.8.refs_1_ = bf16[32,3072]{1,0:T(8,128)(2,1)S(1)} collective-permute-done((bf16[32,3072]{1,0:T(8,128)(2,1)S(1)}, bf16[32,3072]{1,0:T(8,128)(2,1)S(1)}, u32[]{:S(2)}, u32[]{:S(2)}) %collective-permute-start.8) | collective-permute-done | bytes 196640 | tf_op jit(solution)/shard_map/ppermute | solution.py:481
  40.6 8.6 %block.5 = (bf16[32,3072]{1,0:T(8,128)(2,1)S(1)}, bf16[32,3072]{1,0:T(8,128)(2,1)S(1)}, bf16[4,2,64,512]{3,2,1,0:T(8,128)(2,1)}, bf16[4,16,3072]{2,1,0:T(8,128)(2,1)}) custom-call(bf16[32,3072]{1,0:T(8,128)(2,1)S(1)} %enter.3.refs_0_.refs_2_, bf16[32,3072]{1,0:T(8,128)(2,1)S(1)} %collective-permute-done.8.refs_1_, ...), custom_call_target="tpu_custom_call", output_to_operand_aliasing={{2}: (9, {})} | custom-call | flops 2818572288 | bytes 44040192 | tf_op jit(solution)/shard_map/block/pallas_call | solution.py:379
  49.3 1.3 %collective-permute-done.9.other = bf16[32,3072]{1,0:T(8,128)(2,1)S(1)} collective-permute-done((bf16[32,3072]{1,0:T(8,128)(2,1)S(1)}, bf16[32,3072]{1,0:T(8,128)(2,1)S(1)}, u32[]{:S(2)}, u32[]{:S(2)}) %collective-permute-start.9) | collective-permute-done | bytes 196640 | tf_op jit(solution)/shard_map/ppermute | solution.py:481
  51.3 4.3 %collective-permute-done.10.refs_1_ = bf16[16,3072]{1,0:T(8,128)(2,1)S(1)} collective-permute-done((bf16[16,3072]{1,0:T(8,128)(2,1)S(1)}, bf16[16,3072]{1,0:T(8,128)(2,1)S(1)}, u32[]{:S(2)}, u32[]{:S(2)}) %collective-permute-start.10) | collective-permute-done | bytes 98336 | tf_op jit(solution)/shard_map/ppermute | solution.py:481
  55.9 2.1 %collective-permute-start.12 = (bf16[16,3072]{1,0:T(8,128)(2,1)S(1)}, bf16[16,3072]{1,0:T(8,128)(2,1)S(1)}, u32[]{:S(2)}, u32[]{:S(2)}) collective-permute-start(bf16[16,3072]{1,0:T(8,128)(2,1)S(1)} %finish.4.refs_8_), channel_id=1, source_target_pairs={{0,6},{1,7},{2,4},{3,5},{4,10},{5,11},{6,8},{7,9},{8,14},{9,15},{1... | collective-permute-start | bytes 294920 | tf_op jit(solution)/shard_map/ppermute | solution.py:488
  58.0 5.7 %collective-permute-done.11.refs_0_ = bf16[16,3072]{1,0:T(8,128)(2,1)S(1)} collective-permute-done((bf16[16,3072]{1,0:T(8,128)(2,1)S(1)}, bf16[16,3072]{1,0:T(8,128)(2,1)S(1)}, u32[]{:S(2)}, u32[]{:S(2)}) %collective-permute-start.11) | collective-permute-done | bytes 98336 | tf_op jit(solution)/shard_map/ppermute | solution.py:488
  64.8 1.4 %collective-permute-done.13.refs_1_ = bf16[32,3072]{1,0:T(8,128)(2,1)S(1)} collective-permute-done((bf16[32,3072]{1,0:T(8,128)(2,1)S(1)}, bf16[32,3072]{1,0:T(8,128)(2,1)S(1)}, u32[]{:S(2)}, u32[]{:S(2)}) %collective-permute-start.13) | collective-permute-done | bytes 196640 | tf_op jit(solution)/shard_map/ppermute | solution.py:481
  66.2 8.6 %block.6 = (bf16[32,3072]{1,0:T(8,128)(2,1)S(1)}, bf16[32,3072]{1,0:T(8,128)(2,1)S(1)}, bf16[4,2,64,512]{3,2,1,0:T(8,128)(2,1)}, bf16[4,16,3072]{2,1,0:T(8,128)(2,1)}) custom-call(bf16[32,3072]{1,0:T(8,128)(2,1)S(1)} %enter.4.refs_0_.refs_2_, bf16[32,3072]{1,0:T(8,128)(2,1)S(1)} %collective-permute-done.13.refs_1_, ...), custom_call_target="tpu_custom_call", output_to_operand_aliasing={{2}: (9, {}), {3}: (10, {})} | custom-call | flops 2818572288 | bytes 44040192 | tf_op jit(solution)/shard_map/block/pallas_call | solution.py:379
  75.0 1.3 %collective-permute-done.14.other = bf16[32,3072]{1,0:T(8,128)(2,1)S(1)} collective-permute-done((bf16[32,3072]{1,0:T(8,128)(2,1)S(1)}, bf16[32,3072]{1,0:T(8,128)(2,1)S(1)}, u32[]{:S(2)}, u32[]{:S(2)}) %collective-permute-start.14) | collective-permute-done | bytes 196640 | tf_op jit(solution)/shard_map/ppermute | solution.py:481
  76.9 4.3 %collective-permute-done.15.refs_1_ = bf16[16,3072]{1,0:T(8,128)(2,1)S(1)} collective-permute-done((bf16[16,3072]{1,0:T(8,128)(2,1)S(1)}, bf16[16,3072]{1,0:T(8,128)(2,1)S(1)}, u32[]{:S(2)}, u32[]{:S(2)}) %collective-permute-start.15) | collective-permute-done | bytes 98336 | tf_op jit(solution)/shard_map/ppermute | solution.py:481
  82.4 6.7 %collective-permute-done.16.refs_0_ = bf16[16,3072]{1,0:T(8,128)(2,1)S(1)} collective-permute-done((bf16[16,3072]{1,0:T(8,128)(2,1)S(1)}, bf16[16,3072]{1,0:T(8,128)(2,1)S(1)}, u32[]{:S(2)}, u32[]{:S(2)}) %collective-permute-start.16) | collective-permute-done | bytes 98336 | tf_op jit(solution)/shard_map/ppermute | solution.py:488
  90.3 1.4 %collective-permute-done.18.refs_1_ = bf16[32,3072]{1,0:T(8,128)(2,1)S(1)} collective-permute-done((bf16[32,3072]{1,0:T(8,128)(2,1)S(1)}, bf16[32,3072]{1,0:T(8,128)(2,1)S(1)}, u32[]{:S(2)}, u32[]{:S(2)}) %collective-permute-start.18) | collective-permute-done | bytes 196640 | tf_op jit(solution)/shard_map/ppermute | solution.py:481
  91.7 8.5 %block.7 = (bf16[32,3072]{1,0:T(8,128)(2,1)S(1)}, bf16[32,3072]{1,0:T(8,128)(2,1)S(1)}, bf16[4,2,64,512]{3,2,1,0:T(8,128)(2,1)}, bf16[4,16,3072]{2,1,0:T(8,128)(2,1)}) custom-call(bf16[32,3072]{1,0:T(8,128)(2,1)S(1)} %enter.5.refs_0_.refs_2_, bf16[32,3072]{1,0:T(8,128)(2,1)S(1)} %collective-permute-done.18.refs_1_, ...), custom_call_target="tpu_custom_call", output_to_operand_aliasing={{2}: (9, {}), {3}: (10, {})} | custom-call | flops 2818572288 | bytes 44040192 | tf_op jit(solution)/shard_map/block/pallas_call | solution.py:379
  100.5 1.3 %collective-permute-done.19.other = bf16[32,3072]{1,0:T(8,128)(2,1)S(1)} collective-permute-done((bf16[32,3072]{1,0:T(8,128)(2,1)S(1)}, bf16[32,3072]{1,0:T(8,128)(2,1)S(1)}, u32[]{:S(2)}, u32[]{:S(2)}) %collective-permute-start.19) | collective-permute-done | bytes 196640 | tf_op jit(solution)/shard_map/ppermute | solution.py:481
  102.4 4.3 %collective-permute-done.20.refs_1_ = bf16[16,3072]{1,0:T(8,128)(2,1)S(1)} collective-permute-done((bf16[16,3072]{1,0:T(8,128)(2,1)S(1)}, bf16[16,3072]{1,0:T(8,128)(2,1)S(1)}, u32[]{:S(2)}, u32[]{:S(2)}) %collective-permute-start.20) | collective-permute-done | bytes 98336 | tf_op jit(solution)/shard_map/ppermute | solution.py:481
  (39 shorter events, 10.2 us)
Async XLA Ops:
  0.6 11.8 %copy-start = (f32[1,3,3072]{2,0,1:T(1,128)S(1)}, f32[1,3,3072]{2,0,1:T(1,128)}, u32[]{:S(2)}) copy-start(f32[1,3,3072]{2,0,1:T(1,128)} %param.11) | copy-start | bytes 110596
  0.6 11.8 %copy-start.1 = (f32[1,2,128]{2,1,0:T(2,128)S(1)}, f32[1,2,128]{2,1,0:T(2,128)}, u32[]{:S(2)}) copy-start(f32[1,2,128]{2,1,0:T(2,128)} %param.14) | copy-start | bytes 3076
  1.6 10.9 %collective-permute-start = (bf16[16,3072]{1,0:T(8,128)(2,1)S(1)}, bf16[16,3072]{1,0:T(8,128)(2,1)S(1)}, u32[]{:S(2)}, u32[]{:S(2)}) collective-permute-start(bf16[16,3072]{1,0:T(8,128)(2,1)S(1)} %select_bitcast_fusion.refs_0_), channel_id=1, source_target_pairs={{0,1},{1,0},{2,3},{3,2},{4,5},{5,4},{6,7},{7,6},{8,9},{9,8},{10,11... | collective-permute-start | bytes 294920 | tf_op jit(solution)/shard_map/ppermute | solution.py:481
  2.1 10.3 %collective-permute-start.1 = (bf16[16,3072]{1,0:T(8,128)(2,1)S(1)}, bf16[16,3072]{1,0:T(8,128)(2,1)S(1)}, u32[]{:S(2)}, u32[]{:S(2)}) collective-permute-start(bf16[16,3072]{1,0:T(8,128)(2,1)S(1)} %select_bitcast_fusion.refs_0_), channel_id=1, source_target_pairs={{0,2},{1,3},{2,0},{3,1},{4,6},{5,7},{6,4},{7,5},{8,10},{9,11},{10,... | collective-permute-start | bytes 294920 | tf_op jit(solution)/shard_map/ppermute | solution.py:481
  4.7 7.7 %collective-permute-start.2 = (bf16[16,3072]{1,0:T(8,128)(2,1)S(1)}, bf16[16,3072]{1,0:T(8,128)(2,1)S(1)}, u32[]{:S(2)}, u32[]{:S(2)}) collective-permute-start(bf16[16,3072]{1,0:T(8,128)(2,1)S(1)} %select_bitcast_fusion.refs_0_), channel_id=1, source_target_pairs={{0,3},{1,2},{2,1},{3,0},{4,7},{5,6},{6,5},{7,4},{8,11},{9,10},{10,... | collective-permute-start | bytes 294920 | tf_op jit(solution)/shard_map/ppermute | solution.py:481
  10.6 14.3 %collective-permute-start.4 = (bf16[3,16,3072]{2,1,0:T(8,128)(2,1)S(1)}, bf16[3,16,3072]{2,1,0:T(8,128)(2,1)S(1)}, u32[]{:S(2)}, u32[]{:S(2)}) collective-permute-start(bf16[3,16,3072]{2,1,0:T(8,128)(2,1)S(1)} %get-tuple-element.39.refs_2_), channel_id=1, source_target_pairs={{0,2},{1,3},{2,0},{3,1},{4,6},{5,7},{6,4},{7,5},{8,10},{9,11},{10,... | collective-permute-start | bytes 884744 | tf_op jit(solution)/shard_map/ppermute | solution.py:481
  23.4 1.5 %collective-permute-start.3 = (bf16[32,3072]{1,0:T(8,128)(2,1)S(1)}, bf16[32,3072]{1,0:T(8,128)(2,1)S(1)}, u32[]{:S(2)}, u32[]{:S(2)}) collective-permute-start(bf16[32,3072]{1,0:T(8,128)(2,1)S(1)} %get-tuple-element.38), channel_id=1, source_target_pairs={{0,1},{1,0},{2,3},{3,2},{4,5},{5,4},{6,7},{7,6},{8,9},{9,8},{10,11... | collective-permute-start | bytes 589832 | tf_op jit(solution)/shard_map/ppermute | solution.py:481
  25.0 4.9 %collective-permute-start.5 = (bf16[16,3072]{1,0:T(8,128)(2,1)S(1)}, bf16[16,3072]{1,0:T(8,128)(2,1)S(1)}, u32[]{:S(2)}, u32[]{:S(2)}) collective-permute-start(bf16[16,3072]{1,0:T(8,128)(2,1)S(1)} %get-tuple-element.41), channel_id=1, source_target_pairs={{0,2},{1,3},{2,0},{3,1},{4,6},{5,7},{6,4},{7,5},{8,10},{9,11},{10,... | collective-permute-start | bytes 294920 | tf_op jit(solution)/shard_map/ppermute | solution.py:481
  30.0 8.0 %collective-permute-start.6 = (bf16[16,3072]{1,0:T(8,128)(2,1)S(1)}, bf16[16,3072]{1,0:T(8,128)(2,1)S(1)}, u32[]{:S(2)}, u32[]{:S(2)}) collective-permute-start(bf16[16,3072]{1,0:T(8,128)(2,1)S(1)} %finish.3.refs_8_), channel_id=1, source_target_pairs={{0,4},{1,5},{2,6},{3,7},{4,8},{5,9},{6,10},{7,11},{8,12},{9,13},{1... | collective-permute-start | bytes 294920 | tf_op jit(solution)/shard_map/ppermute | solution.py:488
  31.6 7.5 %collective-permute-start.7 = (bf16[16,3072]{1,0:T(8,128)(2,1)S(1)}, bf16[16,3072]{1,0:T(8,128)(2,1)S(1)}, u32[]{:S(2)}, u32[]{:S(2)}) collective-permute-start(bf16[16,3072]{1,0:T(8,128)(2,1)S(1)} %finish.3.refs_8_), channel_id=1, source_target_pairs={{0,6},{1,7},{2,4},{3,5},{4,10},{5,11},{6,8},{7,9},{8,14},{9,15},{1... | collective-permute-start | bytes 294920 | tf_op jit(solution)/shard_map/ppermute | solution.py:488
  39.1 1.5 %collective-permute-start.8 = (bf16[32,3072]{1,0:T(8,128)(2,1)S(1)}, bf16[32,3072]{1,0:T(8,128)(2,1)S(1)}, u32[]{:S(2)}, u32[]{:S(2)}) collective-permute-start(bf16[32,3072]{1,0:T(8,128)(2,1)S(1)} %enter.3.refs_0_.refs_2_), channel_id=1, source_target_pairs={{0,1},{1,0},{2,3},{3,2},{4,5},{5,4},{6,7},{7,6},{8,9},{9,8},{10,11... | collective-permute-start | bytes 589832 | tf_op jit(solution)/shard_map/ppermute | solution.py:481
  49.1 1.5 %collective-permute-start.9 = (bf16[32,3072]{1,0:T(8,128)(2,1)S(1)}, bf16[32,3072]{1,0:T(8,128)(2,1)S(1)}, u32[]{:S(2)}, u32[]{:S(2)}) collective-permute-start(bf16[32,3072]{1,0:T(8,128)(2,1)S(1)} %get-tuple-element.47), channel_id=1, source_target_pairs={{0,1},{1,0},{2,3},{3,2},{4,5},{5,4},{6,7},{7,6},{8,9},{9,8},{10,11... | collective-permute-start | bytes 589832 | tf_op jit(solution)/shard_map/ppermute | solution.py:481
  50.7 4.9 %collective-permute-start.10 = (bf16[16,3072]{1,0:T(8,128)(2,1)S(1)}, bf16[16,3072]{1,0:T(8,128)(2,1)S(1)}, u32[]{:S(2)}, u32[]{:S(2)}) collective-permute-start(bf16[16,3072]{1,0:T(8,128)(2,1)S(1)} %get-tuple-element.49), channel_id=1, source_target_pairs={{0,2},{1,3},{2,0},{3,1},{4,6},{5,7},{6,4},{7,5},{8,10},{9,11},{10,... | collective-permute-start | bytes 294920 | tf_op jit(solution)/shard_map/ppermute | solution.py:481
  55.6 8.0 %collective-permute-start.11 = (bf16[16,3072]{1,0:T(8,128)(2,1)S(1)}, bf16[16,3072]{1,0:T(8,128)(2,1)S(1)}, u32[]{:S(2)}, u32[]{:S(2)}) collective-permute-start(bf16[16,3072]{1,0:T(8,128)(2,1)S(1)} %finish.4.refs_8_), channel_id=1, source_target_pairs={{0,4},{1,5},{2,6},{3,7},{4,8},{5,9},{6,10},{7,11},{8,12},{9,13},{1... | collective-permute-start | bytes 294920 | tf_op jit(solution)/shard_map/ppermute | solution.py:488
  55.9 8.8 %collective-permute-start.12 = (bf16[16,3072]{1,0:T(8,128)(2,1)S(1)}, bf16[16,3072]{1,0:T(8,128)(2,1)S(1)}, u32[]{:S(2)}, u32[]{:S(2)}) collective-permute-start(bf16[16,3072]{1,0:T(8,128)(2,1)S(1)} %finish.4.refs_8_), channel_id=1, source_target_pairs={{0,6},{1,7},{2,4},{3,5},{4,10},{5,11},{6,8},{7,9},{8,14},{9,15},{1... | collective-permute-start | bytes 294920 | tf_op jit(solution)/shard_map/ppermute | solution.py:488
  64.7 1.5 %collective-permute-start.13 = (bf16[32,3072]{1,0:T(8,128)(2,1)S(1)}, bf16[32,3072]{1,0:T(8,128)(2,1)S(1)}, u32[]{:S(2)}, u32[]{:S(2)}) collective-permute-start(bf16[32,3072]{1,0:T(8,128)(2,1)S(1)} %enter.4.refs_0_.refs_2_), channel_id=1, source_target_pairs={{0,1},{1,0},{2,3},{3,2},{4,5},{5,4},{6,7},{7,6},{8,9},{9,8},{10,11... | collective-permute-start | bytes 589832 | tf_op jit(solution)/shard_map/ppermute | solution.py:481
  74.8 1.5 %collective-permute-start.14 = (bf16[32,3072]{1,0:T(8,128)(2,1)S(1)}, bf16[32,3072]{1,0:T(8,128)(2,1)S(1)}, u32[]{:S(2)}, u32[]{:S(2)}) collective-permute-start(bf16[32,3072]{1,0:T(8,128)(2,1)S(1)} %get-tuple-element.53), channel_id=1, source_target_pairs={{0,1},{1,0},{2,3},{3,2},{4,5},{5,4},{6,7},{7,6},{8,9},{9,8},{10,11... | collective-permute-start | bytes 589832 | tf_op jit(solution)/shard_map/ppermute | solution.py:481
  76.3 4.9 %collective-permute-start.15 = (bf16[16,3072]{1,0:T(8,128)(2,1)S(1)}, bf16[16,3072]{1,0:T(8,128)(2,1)S(1)}, u32[]{:S(2)}, u32[]{:S(2)}) collective-permute-start(bf16[16,3072]{1,0:T(8,128)(2,1)S(1)} %get-tuple-element.55), channel_id=1, source_target_pairs={{0,2},{1,3},{2,0},{3,1},{4,6},{5,7},{6,4},{7,5},{8,10},{9,11},{10,... | collective-permute-start | bytes 294920 | tf_op jit(solution)/shard_map/ppermute | solution.py:481
  81.3 7.8 %collective-permute-start.16 = (bf16[16,3072]{1,0:T(8,128)(2,1)S(1)}, bf16[16,3072]{1,0:T(8,128)(2,1)S(1)}, u32[]{:S(2)}, u32[]{:S(2)}) collective-permute-start(bf16[16,3072]{1,0:T(8,128)(2,1)S(1)} %finish.5.refs_8_), channel_id=1, source_target_pairs={{0,4},{1,5},{2,6},{3,7},{4,8},{5,9},{6,10},{7,11},{8,12},{9,13},{1... | collective-permute-start | bytes 294920 | tf_op jit(solution)/shard_map/ppermute | solution.py:488
  81.4 8.8 %collective-permute-start.17 = (bf16[16,3072]{1,0:T(8,128)(2,1)S(1)}, bf16[16,3072]{1,0:T(8,128)(2,1)S(1)}, u32[]{:S(2)}, u32[]{:S(2)}) collective-permute-start(bf16[16,3072]{1,0:T(8,128)(2,1)S(1)} %finish.5.refs_8_), channel_id=1, source_target_pairs={{0,6},{1,7},{2,4},{3,5},{4,10},{5,11},{6,8},{7,9},{8,14},{9,15},{1... | collective-permute-start | bytes 294920 | tf_op jit(solution)/shard_map/ppermute | solution.py:488
  90.2 1.5 %collective-permute-start.18 = (bf16[32,3072]{1,0:T(8,128)(2,1)S(1)}, bf16[32,3072]{1,0:T(8,128)(2,1)S(1)}, u32[]{:S(2)}, u32[]{:S(2)}) collective-permute-start(bf16[32,3072]{1,0:T(8,128)(2,1)S(1)} %enter.5.refs_0_.refs_2_), channel_id=1, source_target_pairs={{0,1},{1,0},{2,3},{3,2},{4,5},{5,4},{6,7},{7,6},{8,9},{9,8},{10,11... | collective-permute-start | bytes 589832 | tf_op jit(solution)/shard_map/ppermute | solution.py:481
  100.3 1.5 %collective-permute-start.19 = (bf16[32,3072]{1,0:T(8,128)(2,1)S(1)}, bf16[32,3072]{1,0:T(8,128)(2,1)S(1)}, u32[]{:S(2)}, u32[]{:S(2)}) collective-permute-start(bf16[32,3072]{1,0:T(8,128)(2,1)S(1)} %get-tuple-element.59), channel_id=1, source_target_pairs={{0,1},{1,0},{2,3},{3,2},{4,5},{5,4},{6,7},{7,6},{8,9},{9,8},{10,11... | collective-permute-start | bytes 589832 | tf_op jit(solution)/shard_map/ppermute | solution.py:481
  101.8 4.9 %collective-permute-start.20 = (bf16[16,3072]{1,0:T(8,128)(2,1)S(1)}, bf16[16,3072]{1,0:T(8,128)(2,1)S(1)}, u32[]{:S(2)}, u32[]{:S(2)}) collective-permute-start(bf16[16,3072]{1,0:T(8,128)(2,1)S(1)} %get-tuple-element.61), channel_id=1, source_target_pairs={{0,2},{1,3},{2,0},{3,1},{4,6},{5,7},{6,4},{7,5},{8,10},{9,11},{10,... | collective-permute-start | bytes 294920 | tf_op jit(solution)/shard_map/ppermute | solution.py:481
